TPU v7x, 512 devices: a whole 4x4x16 slice. The times are simulated.
512 devices in a mesh: row: 16 (over y, x), col: 32 (over z, core).
Axes of the slice: x: 4, y: 4, z: 16, core: 2. Of those that a mesh axis runs over, the one named last changes fastest.
Arguments:
- tensor: float32 [32, 4096, 4096], P(None, 'row', 'col'), may hold values from -82 to 82
- old_factor: float32 [4096, 32], P('row'), may hold values from -0.09375 to 0.09375
- factor_two: float32 [4096, 32], P('col'), may hold values from -0.09375 to 0.09375
- factor_three: float32 [32, 32], replicated, may hold values from -1 to 1
Outputs:
- new_factor: float32 [4096, 32], P('row')
- core: float32 [32, 1024], P(None, 'col')
All inputs are finite; a program needn't handle non-finite values.
Results may differ from a plain program's by a relative error of at most 0.0003.
Values sent between devices are 32-bit elements; how exact they have to be, the bound alone decides.
No kernel may reach another device: no remote copies, remote signals or barrier semaphores. Data moves between devices by JAX's collectives and lax.ppermute only.
A program may use at most 64 MiB of HBM per device.

v0:
```python
import math
import jax
import jax.numpy as jnp
from jax import lax
from jax.sharding import PartitionSpec as P

I1 = 4096
ITERS = 2


def right_solve(lower, matrix):
    return lax.linalg.triangular_solve(lower, matrix, left_side=False, lower=True, transpose_a=True)


def shards(tensor, old_factor, factor_two, factor_three):
    highest = lax.Precision.HIGHEST
    depth, rows, cols = tensor.shape
    rank = factor_three.shape[1]
    third = jnp.dot(factor_three.T, tensor.reshape(depth, rows * cols), precision=highest)
    third = third.reshape(rank, rows, cols)
    partial_value = jnp.einsum("bij,ja->iab", third, factor_two, precision=highest).reshape(
        rows, rank * rank
    )
    unfolded = lax.psum_scatter(partial_value, "col", scatter_dimension=1, tiled=True)

    def project(factor):
        local = jnp.dot(unfolded.T, factor, precision=highest)
        summed = lax.psum(local, "row")
        return summed

    factor = old_factor
    coeffs = project(factor)
    for step in range(ITERS):
        image_local = jnp.dot(unfolded, coeffs, precision=highest)
        image_summed = lax.psum(image_local, "col")
        gram_local = jnp.dot(image_summed.T, image_summed, precision=highest)
        gram = lax.psum(gram_local, "row")
        lower = jnp.linalg.cholesky(gram)
        factor = right_solve(lower, image_summed)
        coeffs = project(factor)
    core = coeffs.T
    return (factor * math.sqrt(I1), core)


def solution(mesh):
    return jax.shard_map(
        shards,
        mesh=mesh,
        in_specs=(P(None, "row", "col"), P("row", None), P("col", None), P()),
        out_specs=(P("row", None), P(None, "col")),
        check_vma=False,
    )
```

profile of v0, /device:TPU:2, one launch (start us, length us, event | category | flops | bytes accessed | tf_op | source)
XLA Modules:
  0.0 694.2 jit_solution(8862657409525127718)
XLA Ops:
  7.2 8.3 %fusion = f32[32,256,128]{2,0,1:T(8,128)S(1)} fusion(f32[32,32]{1,0:T(8,128)} %param.10, f32[4,8,256,128]{3,2,1,0:T(8,128)} %bitcast.65), kind=kOutput, calls=%fused_computation.1 | convolution fusion | flops 402653184 | bytes 8392704 | tf_op jit(solution)/shard_map/dot_general | solution.py:19
  15.6 5.0 convolution_bitcast_fusion
  20.6 4.7 copy.10
  25.3 112.8 %reduce-scatter.2.cloned.1.call-done = f32[256,32]{0,1:T(8,128)} async-done(((f32[256,1024]{0,1:T(8,128)}), f32[256,32]{0,1:T(8,128)}) %reduce-scatter.2.cloned.1.call-update) | async-done | bytes 32784 | tf_op jit(solution)/shard_map/reduce_scatter | solution.py:24
  138.1 0.9 fusion.13
  139.0 69.2 %psum.49 = f32[32,32]{1,0:T(8,128)S(1)} all-reduce(f32[32,32]{1,0:T(8,128)S(1)} %fusion.13), channel_id=1, replica_groups=mesh['row'=16,'col'=32] {'row'}, use_global_device_ids=true, to_apply=%region_1.0 | all-reduce | flops 1024 | bytes 8192 | tf_op jit(solution)/shard_map/psum | solution.py:28
  208.2 1.0 fusion.14
  209.2 90.0 %psum.50 = f32[256,32]{0,1:T(8,128)S(1)} all-reduce(f32[256,32]{0,1:T(8,128)S(1)} %fusion.14), channel_id=1, replica_groups=mesh['row'=16,'col'=32] {'col'}, use_global_device_ids=true, to_apply=%region_2.0 | all-reduce | flops 8192 | bytes 65536 | tf_op jit(solution)/shard_map/psum | solution.py:35
  299.4 71.7 %psum.51 = f32[32,32]{0,1:T(8,128)S(1)} all-reduce(f32[32,32]{0,1:T(8,128)S(1)} %fusion.15), channel_id=1, replica_groups=mesh['row'=16,'col'=32] {'row'}, use_global_device_ids=true, to_apply=%region_3.0 | all-reduce | flops 1024 | bytes 8192 | tf_op jit(solution)/shard_map/psum | solution.py:37
  371.1 2.9 cholesky.44
  374.1 0.6 compare_reduce_fusion.1
  374.7 0.7 fusion.3
  375.4 2.4 custom-call.6
  378.1 0.9 fusion.16
  379.0 69.5 %psum.52 = f32[32,32]{1,0:T(8,128)S(1)} all-reduce(f32[32,32]{1,0:T(8,128)S(1)} %fusion.16), channel_id=1, replica_groups=mesh['row'=16,'col'=32] {'row'}, use_global_device_ids=true, to_apply=%region_6.9 | all-reduce | flops 1024 | bytes 8192 | tf_op jit(solution)/shard_map/psum | solution.py:28
  448.5 1.0 fusion.17
  449.5 90.0 %psum.53 = f32[256,32]{0,1:T(8,128)S(1)} all-reduce(f32[256,32]{0,1:T(8,128)S(1)} %fusion.17), channel_id=1, replica_groups=mesh['row'=16,'col'=32] {'col'}, use_global_device_ids=true, to_apply=%region_7.10 | all-reduce | flops 8192 | bytes 65536 | tf_op jit(solution)/shard_map/psum | solution.py:35
  539.7 69.5 %psum.54 = f32[32,32]{0,1:T(8,128)S(1)} all-reduce(f32[32,32]{0,1:T(8,128)S(1)} %fusion.18), channel_id=1, replica_groups=mesh['row'=16,'col'=32] {'row'}, use_global_device_ids=true, to_apply=%region_8.11 | all-reduce | flops 1024 | bytes 8192 | tf_op jit(solution)/shard_map/psum | solution.py:37
  609.3 2.9 cholesky.55
  612.9 0.7 fusion.4
  613.6 2.4 custom-call.7
  616.0 0.9 broadcast_multiply_fusion
  616.9 0.9 fusion.19
  617.8 69.6 %psum.55 = f32[32,32]{1,0:T(8,128)} all-reduce(f32[32,32]{1,0:T(8,128)S(1)} %fusion.19), channel_id=1, replica_groups=mesh['row'=16,'col'=32] {'row'}, use_global_device_ids=true, to_apply=%region_9.12 | all-reduce | flops 1024 | bytes 8192 | tf_op jit(solution)/shard_map/psum | solution.py:28
  (16 shorter events, 1.5 us)
Async XLA Ops:
  7.2 130.9 %copy-start = (f32[256,32]{0,1:T(8,128)S(1)}, f32[256,32]{0,1:T(8,128)}, u32[]{:S(2)}) copy-start(f32[256,32]{0,1:T(8,128)} %param.8) | copy-start | bytes 98308
  7.2 130.9 %reduce-scatter.2.cloned.1.call-start = ((), (), s32[]{:S(2)}) async-start(), calls=%async_computation.1 | async-start | bytes 1081344 | tf_op jit(solution)/shard_map/reduce_scatter | solution.py:24
  7.2 8.3 %copy-start.1 = (f32[128,32]{0,1:T(8,128)S(1)}, f32[128,32]{0,1:T(8,128)}, u32[]{:S(2)}) copy-start(f32[128,32]{0,1:T(8,128)} %param.9) | copy-start | bytes 49156
Sparse Core Ops, SparseCore 0:
  25.4 112.5 reduce-scatter.1
where the time goes:
time: 695 us; the launch traced here: 694 us
  blocking collectives  530 us (76%)
  waiting for transfers between devices  113 us (16%)
  matrix products  19.4 us (3%)
  between operations  14.1 us (2%)
  other arithmetic  13.4 us (2%)
    psum x3, blocking collectives, project(): summed = lax.psum(local, 'row')  208 us
    psum x2, blocking collectives, shards(): image_summed = lax.psum(image_local, 'col')  180 us
    psum x2, blocking collectives, shards(): gram = lax.psum(gram_local, 'row')  141 us
    reduce_scatter x1, waiting for transfers between devices, shards(): lax.psum_scatter(partial_value, 'col', scatter_dimension=1, tiled=True)  113 us
  transfers between devices with their start and end apart: 1, of which 1 were waited for; matrix products, arithmetic and copies ran while one was open for 0% of the time, Pallas kernels for 0%

commit v1 on v0

--- a/solution.py
+++ b/solution.py
@@ -34,7 +34,7 @@
         image_local = jnp.dot(unfolded, coeffs, precision=highest)
         image_summed = lax.psum(image_local, "col")
         gram_local = jnp.dot(image_summed.T, image_summed, precision=highest)
-        gram = lax.psum(gram_local, "row")
+        gram = jnp.sum(lax.all_gather(gram_local, "row"), axis=0)
         lower = jnp.linalg.cholesky(gram)
         factor = right_solve(lower, image_summed)
         coeffs = project(factor)

time: 695 us -> 602 us (0.87)
  the two profiles are of different devices: /device:TPU:2 before, /device:TPU:32 now
where the time goes in v1:
time: 602 us; the launch traced here: 601 us
  blocking collectives  440 us (73%)
  waiting for transfers between devices  109 us (18%)
  matrix products  19.4 us (3%)
  between operations  14.2 us (2%)
  other arithmetic  13.4 us (2%)
    psum x3, blocking collectives, project(): summed = lax.psum(local, 'row')  218 us
    psum x2, blocking collectives, shards(): image_summed = lax.psum(image_local, 'col')  180 us
    reduce_scatter x1, waiting for transfers between devices, shards(): lax.psum_scatter(partial_value, 'col', scatter_dimension=1, tiled=True)  109 us
    all_gather x2, blocking collectives, shards(): gram = jnp.sum(lax.all_gather(gram_local, 'row'), axis=0)  41.4 us
  transfers between devices with their start and end apart: 1, of which 1 were waited for; matrix products, arithmetic and copies ran while one was open for 0% of the time, Pallas kernels for 0%

profile of v1, /device:TPU:32, one launch (start us, length us, event | category | flops | bytes accessed | tf_op | source)
XLA Modules:
  0.0 601.2 jit_solution(1369672741339839874)
XLA Ops:
  7.2 8.3 %fusion = f32[32,256,128]{2,0,1:T(8,128)S(1)} fusion(f32[32,32]{1,0:T(8,128)} %param.10, f32[4,8,256,128]{3,2,1,0:T(8,128)} %bitcast.66), kind=kOutput, calls=%fused_computation.1 | convolution fusion | flops 402653184 | bytes 8392704 | tf_op jit(solution)/shard_map/dot_general | solution.py:19
  15.6 5.0 convolution_bitcast_fusion
  20.6 4.7 copy.18
  25.3 109.3 %reduce-scatter.2.cloned.1.call-done = f32[256,32]{0,1:T(8,128)} async-done(((f32[256,1024]{0,1:T(8,128)}), f32[256,32]{0,1:T(8,128)}) %reduce-scatter.2.cloned.1.call-update) | async-done | bytes 32784 | tf_op jit(solution)/shard_map/reduce_scatter | solution.py:24
  134.6 0.9 fusion.13
  135.6 74.3 %psum.35 = f32[32,32]{1,0:T(8,128)S(1)} all-reduce(f32[32,32]{1,0:T(8,128)S(1)} %fusion.13), channel_id=1, replica_groups=mesh['row'=16,'col'=32] {'row'}, use_global_device_ids=true, to_apply=%region_1.0 | all-reduce | flops 1024 | bytes 8192 | tf_op jit(solution)/shard_map/psum | solution.py:28
  209.8 1.0 fusion.14
  210.8 90.1 %psum.36 = f32[256,32]{0,1:T(8,128)S(1)} all-reduce(f32[256,32]{0,1:T(8,128)S(1)} %fusion.14), channel_id=1, replica_groups=mesh['row'=16,'col'=32] {'col'}, use_global_device_ids=true, to_apply=%region_2.0 | all-reduce | flops 8192 | bytes 65536 | tf_op jit(solution)/shard_map/psum | solution.py:35
  301.1 20.7 %all-gather = f32[512,32]{1,0:T(8,128)S(1)} all-gather(f32[32,32]{1,0:T(8,128)S(1)} %fusion.15), channel_id=2, replica_groups=mesh['row'=16,'col'=32] {'row'}, dimensions={0}, use_global_device_ids=true | all-gather | bytes 69632 | tf_op jit(solution)/shard_map/all_gather | solution.py:37
  321.9 2.9 cholesky.44
  324.8 0.6 compare_reduce_fusion.1
  325.5 0.7 fusion.3
  326.1 2.4 custom-call.6
  328.8 0.9 fusion.16
  329.8 72.1 %psum.37 = f32[32,32]{1,0:T(8,128)S(1)} all-reduce(f32[32,32]{1,0:T(8,128)S(1)} %fusion.16), channel_id=1, replica_groups=mesh['row'=16,'col'=32] {'row'}, use_global_device_ids=true, to_apply=%region_6.9 | all-reduce | flops 1024 | bytes 8192 | tf_op jit(solution)/shard_map/psum | solution.py:28
  401.8 1.0 fusion.17
  402.8 90.0 %psum.38 = f32[256,32]{0,1:T(8,128)S(1)} all-reduce(f32[256,32]{0,1:T(8,128)S(1)} %fusion.17), channel_id=1, replica_groups=mesh['row'=16,'col'=32] {'col'}, use_global_device_ids=true, to_apply=%region_7.10 | all-reduce | flops 8192 | bytes 65536 | tf_op jit(solution)/shard_map/psum | solution.py:35
  493.0 20.7 %all-gather.1 = f32[512,32]{1,0:T(8,128)S(1)} all-gather(f32[32,32]{1,0:T(8,128)S(1)} %fusion.18), channel_id=3, replica_groups=mesh['row'=16,'col'=32] {'row'}, dimensions={0}, use_global_device_ids=true | all-gather | bytes 69632 | tf_op jit(solution)/shard_map/all_gather | solution.py:37
  513.8 2.9 cholesky.55
  517.4 0.7 fusion.4
  518.1 2.4 custom-call.7
  520.5 0.9 broadcast_multiply_fusion
  521.4 0.9 fusion.19
  522.3 72.1 %psum.39 = f32[32,32]{1,0:T(8,128)} all-reduce(f32[32,32]{1,0:T(8,128)S(1)} %fusion.19), channel_id=1, replica_groups=mesh['row'=16,'col'=32] {'row'}, use_global_device_ids=true, to_apply=%region_9.12 | all-reduce | flops 1024 | bytes 8192 | tf_op jit(solution)/shard_map/psum | solution.py:28
  (18 shorter events, 1.6 us)
Async XLA Ops:
  7.2 127.5 %copy-start = (f32[256,32]{0,1:T(8,128)S(1)}, f32[256,32]{0,1:T(8,128)}, u32[]{:S(2)}) copy-start(f32[256,32]{0,1:T(8,128)} %param.8) | copy-start | bytes 98308
  7.2 127.4 %reduce-scatter.2.cloned.1.call-start = ((), (), s32[]{:S(2)}) async-start(), calls=%async_computation.1 | async-start | bytes 1081344 | tf_op jit(solution)/shard_map/reduce_scatter | solution.py:24
  7.2 8.3 %copy-start.1 = (f32[128,32]{0,1:T(8,128)S(1)}, f32[128,32]{0,1:T(8,128)}, u32[]{:S(2)}) copy-start(f32[128,32]{0,1:T(8,128)} %param.9) | copy-start | bytes 49156
Sparse Core Ops, SparseCore 0:
  25.4 109.1 reduce-scatter.1
